TPU v7x, 128 devices: a whole 4x4x4 slice. The times are simulated.
128 devices in a mesh: ctx: 32 (over z, x, core), ch: 4 (over y).
Axes of the slice: x: 4, y: 4, z: 4, core: 2. Of those that a mesh axis runs over, the one named last changes fastest.
Arguments:
- projections: bfloat16 [3, 4096, 8192], P(None, 'ch', 'ctx'), may hold values from -6 to 6
- short_filter: float32 [3, 4096, 3], P(None, 'ch'), may hold values from -3 to 3
- skip_gain: float32 [4096], P('ch'), may hold values from -1 to 1
- filter_spectra: bfloat16 [2, 4096, 16384], P(None, 'ch', 'ctx'), may hold values from -6 to 6
Outputs:
- gated_output: bfloat16 [4096, 8192], P('ch', 'ctx')
All inputs are finite; a program needn't handle non-finite values.
Results may differ from a plain program's by a relative error of at most 0.0075.
Values may be sent and summed in bfloat16 or wider, within the bound.
A program may use at most 128 MiB of HBM per device.

v0:
```python
import math

import jax
import jax.numpy as jnp
from jax import lax
from jax.sharding import PartitionSpec as P

precise = lax.Precision.HIGHEST


def from_behind(x, axis, by):
    count = lax.axis_size(axis)
    pairs = [(i, i + by) for i in range(count) if 0 <= i + by < count]
    return lax.ppermute(x, axis, pairs)


def phase_table(first, second, period, sign):
    counts = first[:, None] * second[None, :] % period
    theta = sign * 2.0 * math.pi / period * counts.astype(jnp.float32)
    return (jnp.cos(theta), jnp.sin(theta))


def rotate(real_in, imag_in, pattern, cos_tab, sin_tab):
    real_out = jnp.einsum(pattern, real_in, cos_tab, precision=precise) - jnp.einsum(
        pattern, imag_in, sin_tab, precision=precise
    )
    imag_out = jnp.einsum(pattern, real_in, sin_tab, precision=precise) + jnp.einsum(
        pattern, imag_in, cos_tab, precision=precise
    )
    return (real_out, imag_out)


def forward_local(real_in, imag_in):
    total = real_in.shape[-1]
    inner_len = min(total, 128)
    outer_len = total // inner_len
    leading = real_in.shape[:-1]
    real_grid = real_in.reshape(leading + (outer_len, inner_len))
    imag_grid = imag_in.reshape(leading + (outer_len, inner_len))
    outer_idx = jnp.arange(outer_len, dtype=jnp.int32)
    inner_idx = jnp.arange(inner_len, dtype=jnp.int32)
    cos_tab, sin_tab = phase_table(outer_idx, outer_idx, outer_len, -1.0)
    real_one, imag_one = rotate(real_grid, imag_grid, "...ab,ak->...kb", cos_tab, sin_tab)
    cos_tw, sin_tw = phase_table(outer_idx, inner_idx, total, -1.0)
    real_two = real_one * cos_tw - imag_one * sin_tw
    imag_two = real_one * sin_tw + imag_one * cos_tw
    cos_tab, sin_tab = phase_table(inner_idx, inner_idx, inner_len, -1.0)
    real_three, imag_three = rotate(real_two, imag_two, "...kb,bm->...mk", cos_tab, sin_tab)
    return (real_three.reshape(leading + (total,)), imag_three.reshape(leading + (total,)))


def inverse_local(real_in, imag_in):
    total = real_in.shape[-1]
    inner_len = min(total, 128)
    outer_len = total // inner_len
    leading = real_in.shape[:-1]
    real_grid = real_in.reshape(leading + (inner_len, outer_len))
    imag_grid = imag_in.reshape(leading + (inner_len, outer_len))
    outer_idx = jnp.arange(outer_len, dtype=jnp.int32)
    inner_idx = jnp.arange(inner_len, dtype=jnp.int32)
    cos_tab, sin_tab = phase_table(inner_idx, inner_idx, inner_len, 1.0)
    real_one, imag_one = rotate(real_grid, imag_grid, "...mk,mb->...kb", cos_tab, sin_tab)
    cos_tw, sin_tw = phase_table(outer_idx, inner_idx, total, 1.0)
    real_two = real_one * cos_tw - imag_one * sin_tw
    imag_two = real_one * sin_tw + imag_one * cos_tw
    cos_tab, sin_tab = phase_table(outer_idx, outer_idx, outer_len, 1.0)
    real_three, imag_three = rotate(real_two, imag_two, "...kb,ka->...ab", cos_tab, sin_tab)
    return (real_three.reshape(leading + (total,)), imag_three.reshape(leading + (total,)))


def shards(projections, short_filter, skip_gain, filter_spectra):
    channels = short_filter.shape[1]
    ctx_count = lax.axis_size("ctx")
    position = lax.axis_index("ctx")
    piece_len = projections.shape[2]
    blocks = 2 * ctx_count
    period = 2 * piece_len * ctx_count
    proj_local = jnp.transpose(projections, (1, 0, 2))
    earlier = from_behind(proj_local[:, :, -2:], "ctx", 1)
    extended = jnp.concatenate([earlier, proj_local], axis=2).astype(jnp.float32)
    taps = jnp.transpose(short_filter, (1, 0, 2))
    filtered = (
        taps[:, :, 0:1] * extended[:, :, 2:]
        + taps[:, :, 1:2] * extended[:, :, 1:-1]
        + taps[:, :, 2:3] * extended[:, :, :-2]
    )
    query = filtered[:, 0]
    product = (filtered[:, 1] * filtered[:, 2]).astype(jnp.bfloat16)
    sub_len = piece_len // ctx_count
    token_global = position * sub_len + jnp.arange(sub_len, dtype=jnp.int32)
    block_idx = jnp.arange(blocks, dtype=jnp.int32)
    source_idx = jnp.arange(ctx_count, dtype=jnp.int32)
    values = lax.all_to_all(
        product[:, None, :], "ctx", split_axis=2, concat_axis=1, tiled=True
    ).astype(jnp.float32)
    cos_tab, sin_tab = phase_table(block_idx, source_idx, blocks, -1.0)
    real_part = jnp.einsum("ka,naj->nkj", cos_tab, values, precision=precise)
    imag_part = jnp.einsum("ka,naj->nkj", sin_tab, values, precision=precise)
    cos_tw, sin_tw = phase_table(block_idx, token_global, period, -1.0)
    stacked = jnp.stack(
        [real_part * cos_tw - imag_part * sin_tw, real_part * sin_tw + imag_part * cos_tw]
    )
    partial_value = lax.all_to_all(stacked, "ctx", split_axis=2, concat_axis=3, tiled=True)
    spec_real, spec_imag = forward_local(partial_value[0], partial_value[1])
    reordered = lax.all_to_all(
        jnp.stack([spec_real, spec_imag]), "ctx", split_axis=3, concat_axis=2, tiled=True
    )
    natural = jnp.swapaxes(reordered, 2, 3).reshape(2, channels, 2 * piece_len)
    filter_real = filter_spectra[0].astype(jnp.float32)
    filter_imag = filter_spectra[1].astype(jnp.float32)
    shaped_real = natural[0] * filter_real - natural[1] * filter_imag
    shaped_imag = natural[0] * filter_imag + natural[1] * filter_real
    returning = jnp.swapaxes(
        jnp.stack([shaped_real, shaped_imag]).reshape(2, channels, sub_len, blocks), 2, 3
    )
    shaped = lax.all_to_all(returning, "ctx", split_axis=2, concat_axis=3, tiled=True)
    back_real, back_imag = inverse_local(shaped[0], shaped[1])
    gathered = lax.all_to_all(
        jnp.stack([back_real, back_imag]), "ctx", split_axis=3, concat_axis=2, tiled=True
    )
    cos_tw, sin_tw = phase_table(block_idx, token_global, period, 1.0)
    twisted_real = gathered[0] * cos_tw - gathered[1] * sin_tw
    twisted_imag = gathered[0] * sin_tw + gathered[1] * cos_tw
    cos_tab, sin_tab = phase_table(source_idx, block_idx, blocks, 1.0)
    values = jnp.einsum("ak,nkj->naj", cos_tab, twisted_real, precision=precise) - jnp.einsum(
        "ak,nkj->naj", sin_tab, twisted_imag, precision=precise
    )
    long_conv = lax.all_to_all(
        values * (1.0 / period), "ctx", split_axis=1, concat_axis=2, tiled=True
    )[:, 0, :]
    result = query * (long_conv + skip_gain[:, None] * product.astype(jnp.float32))
    return result.astype(jnp.bfloat16)


def solution(mesh):
    return jax.shard_map(
        shards,
        mesh=mesh,
        in_specs=(P(None, "ch", "ctx"), P(None, "ch", None), P("ch"), P(None, "ch", "ctx")),
        out_specs=P("ch", "ctx"),
        check_vma=False,
    )
```

profile of v0, /device:TPU:1, one launch (start us, length us, event | category | flops | bytes accessed | tf_op | source)
XLA Modules:
  0.0 487.4 jit_solution(2995065394303867685)
XLA Ops:
  0.0 1.7 copy.153
  1.8 4.5 collective-permute-start
  7.6 0.9 fusion
  8.6 0.8 copy.274
  10.6 3.7 reduce
  14.3 1.1 reshape.204
  15.5 9.8 %all-to-all-start = ((bf16[32,2,4096]{2,1,0:T(2,128)(2,1)}), bf16[32,2,4096]{2,1,0:T(2,128)(2,1)S(1)}, u32[]{:S(2)}, u32[]{:S(2)}) async-start(bf16[32,2,4096]{2,1,0:T(2,128)(2,1)} %reshape.204), calls=%async_computation | async-start | bytes 1048576 | tf_op jit(solution)/shard_map/all_to_all | solution.py:93
  25.4 11.3 %all-to-all-done = bf16[32,2,4096]{2,1,0:T(2,128)(2,1)S(1)} async-done(((bf16[32,2,4096]{2,1,0:T(2,128)(2,1)}), bf16[32,2,4096]{2,1,0:T(2,128)(2,1)S(1)}, u32[]{:S(2)}, u32[]{:S(2)}) %all-to-all-start) | async-done | bytes 524320 | tf_op jit(solution)/shard_map/all_to_all | solution.py:93
  37.4 1.3 fusion.45
  38.7 1.9 fusion.7
  41.2 4.5 copy.157
  45.6 5.3 %all-to-all-start.1 = ((f32[2,1024,64,8]{1,3,0,2:T(8,128)}), f32[2,1024,64,8]{1,3,0,2:T(8,128)}, u32[]{:S(2)}, u32[]{:S(2)}) async-start(f32[2,1024,64,8]{1,3,0,2:T(8,128)} %copy.157), calls=%async_computation.1 | async-start | bytes 8388608 | tf_op jit(solution)/shard_map/all_to_all | solution.py:103
  50.9 50.0 %all-to-all-done.1 = f32[2,1024,64,8]{1,3,0,2:T(8,128)} async-done(((f32[2,1024,64,8]{1,3,0,2:T(8,128)}), f32[2,1024,64,8]{1,3,0,2:T(8,128)}, u32[]{:S(2)}, u32[]{:S(2)}) %all-to-all-start.1) | async-done | bytes 4194336 | tf_op jit(solution)/shard_map/all_to_all | solution.py:103
  101.0 2.5 copy.158
  103.5 1.8 fusion.222
  105.3 1.5 copy.159
  106.8 3.1 copy.160
  109.9 8.7 %fusion.120 = f32[2,1024,2,128]{3,0,2,1:T(2,128)} fusion(f32[1024,2,2,128]{3,2,1,0:T(2,128)S(1)} %copy.160), kind=kOutput, calls=%fused_computation.165 | convolution fusion | flops 12582968 | bytes 4194304 | tf_op jit(solution)/shard_map/...ab,ak->...kb/dot_general | solution.py:27
  118.5 8.7 %fusion.118 = f32[2,1024,2,128]{3,0,2,1:T(2,128)} fusion(f32[1024,2,2,128]{3,2,1,0:T(2,128)S(1)} %copy.160), kind=kOutput, calls=%fused_computation.163 | convolution fusion | flops 12582968 | bytes 4194304 | tf_op jit(solution)/shard_map/...ab,ak->...kb/dot_general | solution.py:24
  127.4 2.3 copy.162
  129.7 9.9 %convolution_add_fusion = f32[2,1024,2,128]{3,0,2,1:T(2,128)S(1)} fusion(f32[2,1024,2,128]{3,0,2,1:T(2,128)} %fusion.120, f32[1024,2,2,128]{3,2,1,0:T(2,128)} %copy.162), kind=kOutput, calls=%fused_computation.51 | convolution fusion | flops 13107256 | bytes 6291456 | tf_op jit(solution)/shard_map/...ab,ak->...kb/dot_general | solution.py:27
  139.6 9.9 %subtract_bitcast_fusion.2 = (f32[1024,2,2,128]{3,2,1,0:T(2,128)S(1)}, f32[1024,2,2,128]{3,2,1,0:T(2,128)S(1)}) fusion(f32[2,1024,2,128]{3,0,2,1:T(2,128)S(1)} %convolution_add_fusion, f32[2,128]{1,0:T(2,128)S(1)} %get-tuple-element.34, f32[2,128]{1,0:T(2,128)S(1)} %get-tuple-element.35, f32[2,1024,2,128]{3,0,2,1:T(2,128)S(1)} %copy-done.6, ...), kind=kOutput, calls=%fused_computation.42 | convolution fusion | flops 16252984 | bytes 10487808 | tf_op jit(solution)/shard_map/...ab,ak->...kb/dot_general | solution.py:24
  149.5 2.2 fusion.16
  151.7 2.1 fusion.14
  153.9 2.2 subtract_bitcast_fusion.1
  156.1 1.6 copy.169
  157.7 2.2 add_bitcast_fusion.1
  159.9 1.8 copy.174
  161.7 1.8 pad_maximum_fusion.1
  163.5 4.4 copy.175
  167.9 8.0 %all-to-all-start.2 = ((f32[2,1024,2,256]{1,2,0,3:T(2,128)}), f32[2,1024,2,256]{1,2,0,3:T(2,128)}, u32[]{:S(2)}, u32[]{:S(2)}) async-start(f32[2,1024,2,256]{1,2,0,3:T(2,128)} %copy.175), calls=%async_computation.2 | async-start | bytes 8388608 | tf_op jit(solution)/shard_map/all_to_all | solution.py:105
  176.0 1.7 fusion.223
  178.7 47.6 %all-to-all-done.2 = f32[2,1024,2,256]{1,2,0,3:T(2,128)} async-done(((f32[2,1024,2,256]{1,2,0,3:T(2,128)}), f32[2,1024,2,256]{1,2,0,3:T(2,128)}, u32[]{:S(2)}, u32[]{:S(2)}) %all-to-all-start.2) | async-done | bytes 4194336 | tf_op jit(solution)/shard_map/all_to_all | solution.py:105
  226.3 4.6 copy.271
  231.9 1.2 copy.178
  233.1 1.2 copy.180
  234.3 1.1 fusion.2
  235.7 4.5 copy.182
  240.2 8.4 %all-to-all-start.3 = ((f32[2,1024,64,8]{1,3,0,2:T(8,128)}), f32[2,1024,64,8]{1,3,0,2:T(8,128)}, u32[]{:S(2)}, u32[]{:S(2)}) async-start(f32[2,1024,64,8]{1,3,0,2:T(8,128)} %copy.182), calls=%async_computation.3 | async-start | bytes 8388608 | tf_op jit(solution)/shard_map/all_to_all | solution.py:116
  248.6 50.0 %all-to-all-done.3 = f32[2,1024,64,8]{1,3,0,2:T(8,128)} async-done(((f32[2,1024,64,8]{1,3,0,2:T(8,128)}), f32[2,1024,64,8]{1,3,0,2:T(8,128)}, u32[]{:S(2)}, u32[]{:S(2)}) %all-to-all-start.3) | async-done | bytes 4194336 | tf_op jit(solution)/shard_map/all_to_all | solution.py:116
  298.6 2.5 copy.183
  301.1 1.8 fusion.220
  302.9 2.9 copy.184
  305.9 2.8 copy.185
  308.7 3.4 fusion.52
  312.0 3.4 fusion.54
  315.4 3.0 copy.186
  318.4 3.2 copy.187
  321.6 3.9 convolution_subtract_fusion.1
  325.5 2.5 multiply_add_fusion
  327.9 10.3 %fusion.30 = f32[2,1024,2,128]{3,0,2,1:T(2,128)S(1)} fusion(f32[1024,2,2,128]{3,0,2,1:T(8,128)S(1)} %get-tuple-element.12), kind=kOutput, calls=%fused_computation.60 | convolution fusion | flops 12582968 | bytes 4194304 | tf_op jit(solution)/shard_map/...kb,ka->...ab/dot_general | solution.py:24
  338.3 11.4 %fusion.28 = f32[2,1024,2,128]{3,0,2,1:T(2,128)} fusion(f32[1024,2,2,128]{3,0,2,1:T(8,128)S(1)} %get-tuple-element.12), kind=kOutput, calls=%fused_computation.58 | convolution fusion | flops 12582968 | bytes 4194304 | tf_op jit(solution)/shard_map/...kb,ka->...ab/dot_general | solution.py:27
  349.7 12.0 %subtract_bitcast_fusion = f32[1024,2,2,128]{3,2,1,0:T(2,128)} fusion(f32[2,1024,2,128]{3,0,2,1:T(2,128)S(1)} %fusion.30, f32[1024,2,2,128]{3,0,2,1:T(8,128)S(1)} %get-tuple-element.11), kind=kOutput, calls=%fused_computation.36 | convolution fusion | flops 13107256 | bytes 6291456 | tf_op jit(solution)/shard_map/...kb,ka->...ab/dot_general | solution.py:24
  361.7 4.9 copy.219
  366.6 12.9 %add_bitcast_fusion = f32[1024,2,2,128]{3,2,1,0:T(2,128)} fusion(f32[2,1024,2,128]{3,0,2,1:T(2,128)} %fusion.28, f32[1024,2,2,128]{3,0,2,1:T(8,128)} %copy-done.5), kind=kOutput, calls=%fused_computation.35 | convolution fusion | flops 13107256 | bytes 6291456 | tf_op jit(solution)/shard_map/...kb,ka->...ab/dot_general | solution.py:27
  379.4 6.1 %copy.220 = f32[1024,2,2,128]{0,1,3,2:T(2,128)} copy(f32[1024,2,2,128]{3,2,1,0:T(2,128)} %add_bitcast_fusion) | data formatting | bytes 4194304 | tf_op jit(solution)/shard_map/stack;reshape | solution.py:119
  385.6 5.7 %pad_maximum_fusion.2 = f32[2,1024,2,256]{1,2,0,3:T(2,128)} fusion(f32[1,1024,2,256]{1,2,0,3:T(2,128)} %bitcast.208, f32[1,1024,2,256]{1,2,0,3:T(2,128)S(1)} %bitcast.206), kind=kLoop, calls=%fused_computation.3 | loop fusion | flops 1048576 | bytes 8388608 | tf_op jit(solution)/shard_map/stack | solution.py:119
  391.3 8.5 %all-to-all-start.4 = ((f32[2,1024,2,256]{1,2,0,3:T(2,128)}), f32[2,1024,2,256]{1,2,0,3:T(2,128)}, u32[]{:S(2)}, u32[]{:S(2)}) async-start(f32[2,1024,2,256]{1,2,0,3:T(2,128)} %pad_maximum_fusion.2), calls=%async_computation.4 | async-start | bytes 8388608 | tf_op jit(solution)/shard_map/all_to_all | solution.py:118
  399.9 49.9 %all-to-all-done.4 = f32[2,1024,2,256]{1,2,0,3:T(2,128)} async-done(((f32[2,1024,2,256]{1,2,0,3:T(2,128)}), f32[2,1024,2,256]{1,2,0,3:T(2,128)}, u32[]{:S(2)}, u32[]{:S(2)}) %all-to-all-start.4) | async-done | bytes 4194336 | tf_op jit(solution)/shard_map/all_to_all | solution.py:118
  449.8 4.6 copy.270
  456.1 2.5 fusion.10
  458.6 2.6 fusion.38
  461.8 23.7 %all_to_all.84 = f32[1024,32,8]{0,2,1:T(8,128)S(1)} all-to-all(f32[1024,32,8]{0,2,1:T(8,128)S(1)} %copy.203), channel_id=1, replica_groups=mesh['ctx'=32,'ch'=4] {'ctx'}, dimensions={1} | all-to-all | bytes 2097152 | tf_op jit(solution)/shard_map/all_to_all | solution.py:128
  486.0 1.0 copy.204
  (49 shorter events, 9.4 us)
Async XLA Ops:
  0.0 6.3 %copy-start.8 = (f32[3,1024,3]{1,2,0:T(4,128)S(1)}, f32[3,1024,3]{1,2,0:T(4,128)}, u32[]{:S(2)}) copy-start(f32[3,1024,3]{1,2,0:T(4,128)} %param.5) | copy-start | bytes 110596
  1.8 5.3 %collective-permute-start = (bf16[1024,3,2]{0,2,1:T(2,128)(2,1)S(1)}, bf16[1024,3,2]{0,2,1:T(2,128)(2,1)S(1)}, u32[]{:S(2)}, u32[]{:S(2)}) collective-permute-start(bf16[1024,3,2]{0,2,1:T(2,128)(2,1)S(1)} %slice.93), channel_id=1, source_target_pairs={{0,4},{4,8},{8,12},{12,16},{16,20},{20,24},{24,28},{28,32},{32,36}... | collective-permute-start | bytes 36872 | tf_op jit(solution)/shard_map/ppermute | solution.py:14
  8.5 1.6 copy-start
  15.5 21.2 %all-to-all-start = ((bf16[32,2,4096]{2,1,0:T(2,128)(2,1)}), bf16[32,2,4096]{2,1,0:T(2,128)(2,1)S(1)}, u32[]{:S(2)}, u32[]{:S(2)}) async-start(bf16[32,2,4096]{2,1,0:T(2,128)(2,1)} %reshape.204), calls=%async_computation | async-start | bytes 1048576 | tf_op jit(solution)/shard_map/all_to_all | solution.py:93
  45.6 55.4 %all-to-all-start.1 = ((f32[2,1024,64,8]{1,3,0,2:T(8,128)}), f32[2,1024,64,8]{1,3,0,2:T(8,128)}, u32[]{:S(2)}, u32[]{:S(2)}) async-start(f32[2,1024,64,8]{1,3,0,2:T(8,128)} %copy.157), calls=%async_computation.1 | async-start | bytes 8388608 | tf_op jit(solution)/shard_map/all_to_all | solution.py:103
  118.5 8.7 %copy-start.3 = (f32[1,1024,2,32,8]{1,4,2,3,0:T(8,128)S(1)}, f32[1,1024,2,32,8]{1,4,2,3,0:T(8,128)}, u32[]{:S(2)}) copy-start(f32[1,1024,2,32,8]{1,4,2,3,0:T(8,128)} %get-tuple-element.21) | copy-start | bytes 6291460
  129.7 9.9 %copy-start.6 = (f32[2,1024,2,128]{3,0,2,1:T(2,128)S(1)}, f32[2,1024,2,128]{3,0,2,1:T(2,128)}, u32[]{:S(2)}) copy-start(f32[2,1024,2,128]{3,0,2,1:T(2,128)} %fusion.118) | copy-start | bytes 6291460
  129.7 9.9 %copy-start.7 = (f32[1024,2,2,128]{3,2,1,0:T(2,128)S(1)}, f32[1024,2,2,128]{3,2,1,0:T(2,128)}, u32[]{:S(2)}) copy-start(f32[1024,2,2,128]{3,2,1,0:T(2,128)} %copy.162) | copy-start | bytes 6291460
  167.9 58.4 %all-to-all-start.2 = ((f32[2,1024,2,256]{1,2,0,3:T(2,128)}), f32[2,1024,2,256]{1,2,0,3:T(2,128)}, u32[]{:S(2)}, u32[]{:S(2)}) async-start(f32[2,1024,2,256]{1,2,0,3:T(2,128)} %copy.175), calls=%async_computation.2 | async-start | bytes 8388608 | tf_op jit(solution)/shard_map/all_to_all | solution.py:105
  240.2 58.5 %all-to-all-start.3 = ((f32[2,1024,64,8]{1,3,0,2:T(8,128)}), f32[2,1024,64,8]{1,3,0,2:T(8,128)}, u32[]{:S(2)}, u32[]{:S(2)}) async-start(f32[2,1024,64,8]{1,3,0,2:T(8,128)} %copy.182), calls=%async_computation.3 | async-start | bytes 8388608 | tf_op jit(solution)/shard_map/all_to_all | solution.py:116
  312.0 3.4 copy-start.4
  321.6 3.9 copy-start.2
  327.9 21.8 %copy-start.5 = (f32[1024,2,2,128]{3,0,2,1:T(8,128)}, f32[1024,2,2,128]{3,0,2,1:T(8,128)S(1)}, u32[]{:S(2)}) copy-start(f32[1024,2,2,128]{3,0,2,1:T(8,128)S(1)} %get-tuple-element.11) | copy-start | bytes 6291460
  391.3 58.6 %all-to-all-start.4 = ((f32[2,1024,2,256]{1,2,0,3:T(2,128)}), f32[2,1024,2,256]{1,2,0,3:T(2,128)}, u32[]{:S(2)}, u32[]{:S(2)}) async-start(f32[2,1024,2,256]{1,2,0,3:T(2,128)} %pad_maximum_fusion.2), calls=%async_computation.4 | async-start | bytes 8388608 | tf_op jit(solution)/shard_map/all_to_all | solution.py:118
  461.2 24.3 %copy-start.1 = (f32[1024,3,256]{0,2,1:T(8,128)S(1)}, f32[1024,3,256]{0,2,1:T(8,128)}, u32[]{:S(2)}) copy-start(f32[1024,3,256]{0,2,1:T(8,128)} %copy-done) | copy-start | bytes 9437188
  461.2 24.3 %copy-start.9 = (f32[1024]{0:T(1024)S(1)}, f32[1024]{0:T(1024)}, u32[]{:S(2)}) copy-start(f32[1024]{0:T(1024)} %param.6) | copy-start | bytes 12292
where the time goes:
time: 494 us; the launch traced here: 487 us
  waiting for transfers between devices  210 us (43%)
  matrix products  114 us (23%)
  local copies, waits for them, and re-layouts  79 us (16%)
  starting transfers between devices  44.3 us (9%)
  blocking collectives  23.7 us (5%)
  other arithmetic  15.9 us (3%)
    all_to_all x1, waiting for transfers between devices, shards(): lax.all_to_all(stacked, 'ctx', split_axis=2, concat_axis=3, tiled=True)  50 us
    all_to_all x1, waiting for transfers between devices, shards(): lax.all_to_all(returning, 'ctx', split_axis=2, concat_axis=3, tiled=True)  50 us
    all_to_all x1, waiting for transfers between devices, shards(): lax.all_to_all(jnp.stack([back_real, back_imag]), 'ctx', split_axis=3, co...  49.9 us
    all_to_all x1, waiting for transfers between devices, shards(): lax.all_to_all(jnp.stack([spec_real, spec_imag]), 'ctx', split_axis=3, co...  47.6 us
    dot_general x4, matrix products, rotate(): jnp.einsum(pattern, imag_in, sin_tab, precision=precise)  27.9 us
    dot_general x4, matrix products, rotate(): jnp.einsum(pattern, imag_in, cos_tab, precision=precise)  27.4 us
    dot_general x4, matrix products, rotate(): jnp.einsum(pattern, real_in, sin_tab, precision=precise)  25.7 us
    dot_general x4, matrix products, rotate(): jnp.einsum(pattern, real_in, cos_tab, precision=precise)  24.6 us
  transfers between devices with their start and end apart: 6, of which 6 were waited for; matrix products, arithmetic and copies ran while one was open for 1% of the time, Pallas kernels for 0%

commit v1 on v0

v1 whole, which is shorter than its diff:
```python
import functools

import jax
import jax.numpy as jnp
import ml_dtypes
import numpy as np
from jax import lax
from jax.experimental import pallas as pl
from jax.experimental.pallas import tpu as pltpu
from jax.sharding import PartitionSpec as P

MESH = pl.DeviceIdType.MESH
SIDE = 128
GROUP = 8
f32, bf16 = jnp.float32, jnp.bfloat16


def tables(n, own, s_lo, a_lo):
    period = SIDE * SIDE
    groups = own // GROUP
    cols = 2 * a_lo
    order_f = np.zeros((own * cols, own * cols))
    c, j = np.meshgrid(np.arange(own), np.arange(cols), indexing="ij")
    order_f[(c * cols + j).ravel(), (j * own + c).ravel()] = 1
    order_x = np.zeros((SIDE * s_lo, SIDE * s_lo))
    c, s = np.meshgrid(np.arange(SIDE), np.arange(s_lo), indexing="ij")
    order_x[(c * s_lo + s).ravel(), (s * SIDE + c).ravel()] = 1
    order_y = np.zeros((SIDE * s_lo, SIDE * s_lo))
    pairs = SIDE // GROUP
    q, c, s = np.meshgrid(np.arange(pairs), np.arange(GROUP), np.arange(s_lo), indexing="ij")
    order_y[(s * SIDE + q * GROUP + c).ravel(), ((q * GROUP + c) * s_lo + s).ravel()] = 1
    q, part, al = (v.ravel() for v in np.meshgrid(np.arange(n), np.arange(2), np.arange(a_lo), indexing="ij"))
    angle = 2 * np.pi * ((q * a_lo + al)[:, None] * np.arange(SIDE)[None, :] % SIDE) / SIDE
    wr, wi = np.cos(angle), -np.sin(angle)
    sign = np.where(part == 1, -1.0, 1.0)[:, None]
    forward = np.concatenate([np.concatenate([wr, -wi], 1), np.concatenate([wi, wr], 1) * sign], 0)
    vr, vi = np.cos(angle).T, np.sin(angle).T
    real = (part == 0)[None, :]
    inverse = np.concatenate([np.where(real, vr, -vi), np.where(real, vi, vr)], 0)
    small = np.concatenate([order_f, order_x, order_y, forward, inverse], 0)
    s = np.arange(n * s_lo)
    angle = 2 * np.pi * (s[:, None] * np.arange(SIDE)[None, :] % SIDE) / SIDE
    first = np.zeros((n, GROUP, s_lo, GROUP, 2, SIDE))
    last = np.zeros((n, GROUP, s_lo, GROUP, 2, SIDE))
    for g in range(GROUP):
        first[:, g, :, g, 0] = np.cos(angle).reshape(n, s_lo, SIDE)
        first[:, g, :, g, 1] = -np.sin(angle).reshape(n, s_lo, SIDE)
        last[:, g, :, g, 0] = np.cos(angle).reshape(n, s_lo, SIDE) / period
        last[:, g, :, g, 1] = -np.sin(angle).reshape(n, s_lo, SIDE) / period
    shape = (n * GROUP * s_lo, GROUP * 2 * SIDE)
    angle = 2 * np.pi * np.arange(SIDE)[:, None] * np.arange(SIDE)[None, :] / period
    twiddle = np.concatenate([np.cos(angle), np.sin(angle)], 0)
    tail = np.zeros((3, 16, SIDE))
    edge = np.zeros((16, 3, 2, SIDE))
    for e in range(3):
        tail[e, 2 * e, SIDE - 2] = 1
        tail[e, 2 * e + 1, SIDE - 1] = 1
        edge[2 * e + 1, e, 0, 0] = 1
        edge[2 * e, e, 1, 0] = 1
        edge[2 * e + 1, e, 1, 1] = 1
    return [
        small.astype(ml_dtypes.bfloat16),
        twiddle.astype(np.float32),
        first.reshape(shape).astype(ml_dtypes.bfloat16),
        last.reshape(shape).astype(ml_dtypes.bfloat16),
        tail.reshape(48, SIDE).astype(ml_dtypes.bfloat16),
        edge.reshape(16, 6 * SIDE).astype(ml_dtypes.bfloat16),
    ]


def peer(me, o):
    z, x, c = me // 8, (me // 2) % 4, me % 2
    return (z + o // 8) % 4 * 8 + (x + o // 2) % 4 * 2 + (c + o) % 2


def dot(a, b):
    return jnp.dot(a, b, preferred_element_type=f32)


def dot_nt(a, b):
    return lax.dot_general(a, b, (((1,), (1,)), ((), ())), preferred_element_type=f32)


def dot_tn(a, b):
    return lax.dot_general(a, b, (((0,), (0,)), ((), ())), preferred_element_type=f32)


def kernel(
    n, own, s_lo, a_lo,
    filt_hbm, proj_hbm, taps_hbm, skip, small_hbm, twiddle_hbm, first_hbm, last_hbm, tail, edge,
    out,
    filt, proj, taps, small, twiddle, first, last,
    fsend, fbuf, xsend, xbuf, ysend, ybuf, spec, back, conv, query, direct, halo_out, halo_in,
    load_sem, own_sem, fsend_sem, frecv_sem, xsend_sem, xrecv_sem, ysend_sem, yrecv_sem, hsend_sem, hrecv_sem,
):
    me = lax.axis_index("ctx")
    groups = own // GROUP
    cols = 2 * a_lo
    xrows = GROUP * s_lo
    frows = GROUP * cols
    blocks = n * own // SIDE
    per_block = SIDE // own

    loads = [
        pltpu.make_async_copy(src, dst, load_sem.at[i])
        for i, (src, dst) in enumerate(
            [(small_hbm, small), (filt_hbm, filt), (proj_hbm, proj), (taps_hbm, taps), (twiddle_hbm, twiddle), (first_hbm, first), (last_hbm, last)]
        )
    ]
    for load in loads:
        load.start()

    barrier = pltpu.get_barrier_semaphore()

    def greet(i, carry):
        pl.semaphore_signal(barrier, inc=1, device_id={"ctx": peer(me, i)}, device_id_type=MESH)
        return carry

    lax.fori_loop(1, n, greet, 0)

    order_f = small.at[pl.ds(0, 256)]
    order_x = small.at[pl.ds(256, 256)]
    order_y = small.at[pl.ds(512, 256)]
    forward = small.at[pl.ds(768, 512)]
    inverse = small.at[pl.ds(1280, 256)]

    loads[0].wait()
    loads[1].wait()

    def arrange(d, carry):
        rows = pl.ds(pl.multiple_of(d * own, own), own)
        stacked = jnp.concatenate(
            [filt[part, rows, al * SIDE : (al + 1) * SIDE] for part in range(2) for al in range(a_lo)], axis=0
        )
        fsend[d] = dot(order_f[...], stacked).astype(bf16)
        return carry

    lax.fori_loop(0, n, arrange, 0)
    own_f = pltpu.make_async_copy(fsend.at[me], fbuf.at[me], own_sem.at[0])
    own_f.start()

    loads[2].wait()
    halo_out[...] = sum(
        dot_nt(tail[16 * e : 16 * e + 16, :], proj[e, :, (s_lo - 1) * SIDE : s_lo * SIDE]) for e in range(3)
    ).astype(bf16)

    pl.semaphore_wait(barrier, n - 1)

    halo = pltpu.make_async_remote_copy(
        src_ref=halo_out, dst_ref=halo_in, send_sem=hsend_sem, recv_sem=hrecv_sem,
        device_id={"ctx": (me + 1) % n}, device_id_type=MESH,
    )
    halo.start()

    def f_copy(g, d):
        rows = pl.ds(pl.multiple_of(g * frows, frows), frows)
        return pltpu.make_async_remote_copy(
            src_ref=fsend.at[d, rows], dst_ref=fbuf.at[me, rows], send_sem=fsend_sem.at[g], recv_sem=frecv_sem.at[g],
            device_id={"ctx": d}, device_id_type=MESH,
        )

    def f_all(g):
        rows = pl.ds(pl.multiple_of(g * frows, frows), frows)
        return pltpu.make_async_remote_copy(
            src_ref=fsend.at[pl.ds(0, n - 1), rows], dst_ref=fbuf.at[pl.ds(0, n - 1), rows],
            send_sem=fsend_sem.at[g], recv_sem=frecv_sem.at[g], device_id={"ctx": (me + 1) % n}, device_id_type=MESH,
        )

    def f_start(g):
        def one(i, carry):
            f_copy(g, peer(me, i * 11 % n)).start()
            return carry

        lax.fori_loop(1, n, one, 0)

    f_start(0)

    loads[3].wait()
    halo.wait_recv()
    lane = lax.broadcasted_iota(jnp.int32, (SIDE, SIDE), 1)
    eye = lax.broadcasted_iota(jnp.int32, (SIDE, SIDE), 0) == lane
    inside = jnp.where(me == 0, 0.0, 1.0).astype(f32)

    def gate(blk, carry):
        rows = pl.ds(pl.multiple_of(blk * SIDE, SIDE), SIDE)
        edges = dot_tn(halo_in[:, rows], edge[...]) * inside
        filtered = []
        for e in range(3):
            x = proj[e, rows, :].astype(f32)
            back1, back2 = pltpu.roll(x, 1, 1), pltpu.roll(x, 2, 1)
            at = 2 * SIDE * e
            back1 = jnp.concatenate([jnp.where(lane < 1, edges[:, at : at + SIDE], back1[:, :SIDE]), back1[:, SIDE:]], axis=1)
            back2 = jnp.concatenate(
                [jnp.where(lane < 2, edges[:, at + SIDE : at + 2 * SIDE], back2[:, :SIDE]), back2[:, SIDE:]], axis=1
            )
            tap = taps[e, rows, :]
            filtered.append(tap[:, 0:1] * x + tap[:, 1:2] * back1 + tap[:, 2:3] * back2)
        product = (filtered[1] * filtered[2]).astype(bf16)
        gain = jnp.sum(jnp.where(eye, skip[pl.ds(blk, 1), :], 0.0), axis=1, keepdims=True)
        query[rows, :] = filtered[0]
        direct[rows, :] = gain * product.astype(f32)
        stacked = jnp.concatenate([product[:, s * SIDE : (s + 1) * SIDE] for s in range(s_lo)], axis=0)
        arranged = dot(order_x[...], stacked).astype(bf16)
        xsend[pl.ds(pl.multiple_of(blk * per_block, per_block), per_block)] = arranged.reshape(per_block, own * s_lo, SIDE)
        return carry

    lax.fori_loop(0, blocks, gate, 0)

    def x_copy(d):
        return pltpu.make_async_remote_copy(
            src_ref=xsend.at[d], dst_ref=xbuf.at[me], send_sem=xsend_sem, recv_sem=xrecv_sem,
            device_id={"ctx": d}, device_id_type=MESH,
        )

    x_all = pltpu.make_async_remote_copy(
        src_ref=xsend.at[pl.ds(0, n - 1)], dst_ref=xbuf.at[pl.ds(0, n - 1)], send_sem=xsend_sem, recv_sem=xrecv_sem,
        device_id={"ctx": (me + 1) % n}, device_id_type=MESH,
    )

    def x_start(i, carry):
        x_copy(peer(me, i * 11 % n)).start()
        return carry

    lax.fori_loop(1, n, x_start, 0)
    own_x = pltpu.make_async_copy(xsend.at[me], xbuf.at[me], own_sem.at[1])
    own_x.start()

    for g in range(1, groups):
        f_start(g)

    for load in loads[4:]:
        load.wait()
    own_x.wait()
    x_all.wait_recv()
    cos, sin = twiddle[0:SIDE, :], twiddle[SIDE : 2 * SIDE, :]

    for g in range(groups):
        turned = xbuf[:, g * xrows : (g + 1) * xrows, :].reshape(n * xrows, SIDE).T

        def over_s(cp, carry, g=g, turned=turned):
            part = dot(turned, first[:, pl.ds(pl.multiple_of(cp * 4 * SIDE, 4 * SIDE), 4 * SIDE)])
            for c in range(2):
                re, im = part[:, 2 * c * SIDE : (2 * c + 1) * SIDE], part[:, (2 * c + 1) * SIDE : (2 * c + 2) * SIDE]
                spec[g * GROUP // 2 + cp, 0:SIDE, c * SIDE : (c + 1) * SIDE] = (re * cos + im * sin).astype(bf16)
                spec[g * GROUP // 2 + cp, SIDE : 2 * SIDE, c * SIDE : (c + 1) * SIDE] = (im * cos - re * sin).astype(bf16)
            return carry

        lax.fori_loop(0, GROUP // 2, over_s, 0)

    own_f.wait()
    half = n * cols

    def y_copy(g, d):
        return pltpu.make_async_remote_copy(
            src_ref=ysend.at[g, pl.ds(pl.multiple_of(d * xrows, xrows), xrows)],
            dst_ref=ybuf.at[g, pl.ds(pl.multiple_of(me * xrows, xrows), xrows)],
            send_sem=ysend_sem.at[g], recv_sem=yrecv_sem.at[g], device_id={"ctx": d}, device_id_type=MESH,
        )

    def y_all(g):
        return pltpu.make_async_remote_copy(
            src_ref=ysend.at[g, pl.ds(0, (n - 1) * xrows)], dst_ref=ybuf.at[g, pl.ds(0, (n - 1) * xrows)],
            send_sem=ysend_sem.at[g], recv_sem=yrecv_sem.at[g], device_id={"ctx": (me + 1) % n}, device_id_type=MESH,
        )

    own_y = []
    for g in range(groups):
        f_all(g).wait_recv()

        def through(cp, carry, g=g):
            values = dot(forward[...], spec[g * GROUP // 2 + cp])
            taken = fbuf[:, pl.ds(pl.multiple_of(g * frows + cp * 2 * cols, 2 * cols), 2 * cols), :].astype(f32)
            shaped = []
            for c in range(2):
                gains = taken[:, c * cols : (c + 1) * cols, :]
                straight = values[:half, c * SIDE : (c + 1) * SIDE].reshape(n, cols, SIDE) * gains
                crossed = values[half:, c * SIDE : (c + 1) * SIDE].reshape(n, cols, SIDE) * gains
                shaped.append((straight + pltpu.roll(crossed, a_lo, 1)).reshape(half, SIDE).astype(bf16))
            values = dot(inverse[...], jnp.concatenate(shaped, axis=1))
            for c in range(2):
                re, im = values[:SIDE, c * SIDE : (c + 1) * SIDE], values[SIDE:, c * SIDE : (c + 1) * SIDE]
                at = pl.multiple_of(cp * 4 * SIDE, 4 * SIDE) + 2 * c * SIDE
                back[:, pl.ds(pl.multiple_of(at, SIDE), SIDE)] = (re * cos - im * sin).astype(bf16)
                back[:, pl.ds(pl.multiple_of(at + SIDE, SIDE), SIDE)] = (re * sin + im * cos).astype(bf16)
            return carry

        lax.fori_loop(0, GROUP // 2, through, 0)
        ysend[g] = dot_nt(last[...], back[...]).astype(bf16)

        def y_start(i, carry, g=g):
            y_copy(g, peer(me, i * 11 % n)).start()
            return carry

        lax.fori_loop(1, n, y_start, 0)
        mine = pl.ds(pl.multiple_of(me * xrows, xrows), xrows)
        own_y.append(pltpu.make_async_copy(ysend.at[g, mine], ybuf.at[g, mine], own_sem.at[2 + g]))
        own_y[g].start()

    pairs = SIDE // GROUP
    for g in range(groups):
        own_y[g].wait()
        y_all(g).wait_recv()
        for h in range(n // pairs):
            arranged = dot(order_y[...], ybuf[g, h * pairs * xrows : (h + 1) * pairs * xrows, :])
            for s in range(s_lo):
                conv[h * pairs : (h + 1) * pairs, g * GROUP : (g + 1) * GROUP, s * SIDE : (s + 1) * SIDE] = arranged[
                    s * SIDE : (s + 1) * SIDE, :
                ].reshape(pairs, GROUP, SIDE)

    def finish(blk, carry):
        rows = pl.ds(pl.multiple_of(blk * SIDE, SIDE), SIDE)
        values = conv[pl.ds(pl.multiple_of(blk * per_block, per_block), per_block)].reshape(SIDE, s_lo * SIDE)
        out[rows, :] = (query[rows, :] * (values + direct[rows, :])).astype(bf16)
        return carry

    lax.fori_loop(0, blocks, finish, 0)

    halo.wait_send()
    x_all.wait_send()
    for g in range(groups):
        f_all(g).wait_send()
        y_all(g).wait_send()


def shards(projections, short_filter, skip_gain, filter_spectra):
    n = lax.axis_size("ctx")
    channels, tokens = projections.shape[1:]
    freqs = filter_spectra.shape[2]
    own, s_lo, a_lo = channels // n, tokens // SIDE, freqs // SIDE
    groups = own // GROUP
    cols = 2 * a_lo
    anywhere, vmem = pl.BlockSpec(memory_space=pl.ANY), pl.BlockSpec(memory_space=pltpu.VMEM)
    small, twiddle, first, last, tail, edge = tables(n, own, s_lo, a_lo)
    dma = pltpu.SemaphoreType.DMA
    return pl.pallas_call(
        functools.partial(kernel, n, own, s_lo, a_lo),
        out_shape=jax.ShapeDtypeStruct((channels, tokens), bf16),
        in_specs=[anywhere, anywhere, anywhere, vmem, anywhere, anywhere, anywhere, anywhere, vmem, vmem],
        out_specs=vmem,
        scratch_shapes=[
            pltpu.VMEM(filter_spectra.shape, bf16),
            pltpu.VMEM(projections.shape, bf16),
            pltpu.VMEM(short_filter.shape, f32),
            pltpu.VMEM(small.shape, bf16),
            pltpu.VMEM(twiddle.shape, f32),
            pltpu.VMEM(first.shape, bf16),
            pltpu.VMEM(last.shape, bf16),
            pltpu.VMEM((n, own * cols, SIDE), bf16),
            pltpu.VMEM((n, own * cols, SIDE), bf16),
            pltpu.VMEM((n, own * s_lo, SIDE), bf16),
            pltpu.VMEM((n, own * s_lo, SIDE), bf16),
            pltpu.VMEM((groups, n * GROUP * s_lo, SIDE), bf16),
            pltpu.VMEM((groups, n * GROUP * s_lo, SIDE), bf16),
            pltpu.VMEM((own // 2, 2 * SIDE, 2 * SIDE), bf16),
            pltpu.VMEM((SIDE, GROUP * 2 * SIDE), bf16),
            pltpu.VMEM((n, own, tokens), f32),
            pltpu.VMEM((channels, tokens), f32),
            pltpu.VMEM((channels, tokens), f32),
            pltpu.VMEM((16, channels), bf16),
            pltpu.VMEM((16, channels), bf16),
            dma((7,)),
            dma((2 + groups,)),
            dma((groups,)),
            dma((groups,)),
            dma,
            dma,
            dma((groups,)),
            dma((groups,)),
            dma,
            dma,
        ],
        compiler_params=pltpu.CompilerParams(collective_id=0, has_side_effects=True, vmem_limit_bytes=52 << 20),
        cost_estimate=pl.CostEstimate(flops=6_000_000_000, bytes_accessed=12_000_000, transcendentals=0),
    )(
        filter_spectra, projections, short_filter, skip_gain.reshape(channels // SIDE, SIDE),
        small, twiddle, first, last, tail, edge,
    )


def solution(mesh):
    return jax.shard_map(
        shards,
        mesh=mesh,
        in_specs=(P(None, "ch", "ctx"), P(None, "ch", None), P("ch"), P(None, "ch", "ctx")),
        out_specs=P("ch", "ctx"),
        check_vma=False,
    )
```

time: 494 us -> 63.4 us (0.13); the launches traced: 487 us -> 63 us
  waiting for transfers between devices: 210 us -> 0 us
  matrix products: 114 us -> 0 us
  local copies, waits for them, and re-layouts: 79 us -> 7.43 us
  Pallas kernels: 0 us -> 55.6 us
  starting transfers between devices: 44.3 us -> 0 us
  blocking collectives: 23.7 us -> 0 us
  other arithmetic: 15.9 us -> 0 us
    all_to_all x5 -> x0, waiting for transfers between devices: 209 us -> none  [the longest x1 50 us: shards(): lax.all_to_all(stacked, 'ctx', split_axis=2, concat_axis=3, tiled=True)]
    dot_general x20 -> x0, matrix products: 114 us -> none  [the longest x4 27.9 us: rotate(): jnp.einsum(pattern, imag_in, sin_tab, precision=precise)]
    pallas_call x0 -> x1, Pallas kernels: none -> 55.6 us  [shards(): pl.pallas_call(functools.partial(kernel, n, own, s_lo, a_lo), out_shape=j...]
    all_to_all x5 -> x0, starting transfers between devices: 39.8 us -> none  [the longest x1 9.76 us: shards(): lax.all_to_all(product[:, None, :], 'ctx', split_axis=2, concat_axis=1, t...]
    another operation x8 -> x0, local copies, waits for them, and re-layouts: 31.2 us -> none  [the longest x2 11 us: shards(): jnp.stack([back_real, back_imag])]
    all_to_all x1 -> x0, blocking collectives: 23.7 us -> none  [shards(): lax.all_to_all(values * (1.0 / period), 'ctx', split_axis=1, concat_axis=...]
    slice x15 -> x0, local copies, waits for them, and re-layouts: 16.7 us -> none  [the longest x3 7.74 us: shards(): back_real, back_imag = inverse_local(shaped[0], shaped[1])]
    all_to_all x5 -> x0, local copies, waits for them, and re-layouts: 14.8 us -> none  [the longest x2 5.19 us: shards(): lax.all_to_all(jnp.stack([spec_real, spec_imag]), 'ctx', split_axis=3, co...]
  transfers between devices with their start and end apart: 6 -> 0, of which waited for: 6 -> 0; matrix products, arithmetic and copies ran while one was open for 1% -> 0% of each run, Pallas kernels for 0% -> 0%
where the time goes in v1:
time: 63.4 us; the launch traced here: 63 us
  Pallas kernels  55.6 us (88%)
  local copies, waits for them, and re-layouts  7.43 us (12%)
    pallas_call x1, Pallas kernels, shards(): pl.pallas_call(functools.partial(kernel, n, own, s_lo, a_lo), out_shape=j...  55.6 us
    unnamed x12, local copies, waits for them, and re-layouts  7.43 us

profile of v1, /device:TPU:1, one launch (start us, length us, event | category | flops | bytes accessed | tf_op | source)
XLA Modules:
  0.0 63.0 jit_solution(4120150837486301694)
XLA Ops:
  0.0 2.5 %copy.11.taps_hbm = f32[3,1024,3]{2,1,0:T(8,128)} copy(f32[3,1024,3]{1,2,0:T(4,128)} %param.11) | data formatting | bytes 73728 | tf_op args[1]
  2.5 0.0 copy-start
  2.5 0.7 %copy-done = f32[1024]{0:T(1024)S(1)} copy-done((f32[1024]{0:T(1024)S(1)}, f32[1024]{0:T(1024)}, u32[]{:S(2)}) %copy-start) | copy-done | bytes 4120
  3.2 0.0 copy-start.1
  3.2 1.1 %copy-done.1 = bf16[1536,256]{1,0:T(8,128)(2,1)S(1)} copy-done((bf16[1536,256]{1,0:T(8,128)(2,1)S(1)}, bf16[1536,256]{1,0:T(8,128)(2,1)}, u32[]{:S(2)}) %copy-start.1) | copy-done | bytes 786456
  4.3 0.0 copy-start.2
  4.3 0.9 %copy-done.2 = f32[256,128]{1,0:T(8,128)S(1)} copy-done((f32[256,128]{1,0:T(8,128)S(1)}, f32[256,128]{1,0:T(8,128)}, u32[]{:S(2)}) %copy-start.2) | copy-done | bytes 131096
  5.2 0.0 copy-start.3
  5.2 0.7 %copy-done.3 = bf16[16,768]{1,0:T(8,128)(2,1)S(1)} copy-done((bf16[16,768]{1,0:T(8,128)(2,1)S(1)}, bf16[16,768]{1,0:T(8,128)(2,1)}, u32[]{:S(2)}) %copy-start.3) | copy-done | bytes 24600
  5.9 0.0 copy-start.4
  5.9 0.7 %copy-done.4 = bf16[48,128]{1,0:T(8,128)(2,1)S(1)} copy-done((bf16[48,128]{1,0:T(8,128)(2,1)S(1)}, bf16[48,128]{1,0:T(8,128)(2,1)}, u32[]{:S(2)}) %copy-start.4) | copy-done | bytes 12312
  6.6 55.6 %shard_map.100 = bf16[1024,256]{1,0:T(8,128)(2,1)S(1)} custom-call(bf16[2,1024,512]{2,1,0:T(8,128)(2,1)} %filt_hbm.1, bf16[3,1024,256]{2,1,0:T(8,128)(2,1)} %proj_hbm.1, f32[3,1024,3]{2,1,0:T(8,128)} %copy.11.taps_hbm, f32[8,128]{1,0:T(8,128)S(1)} %bitcast.1, bf16[1536,256]{1,0:T(8,128)(2,1)S(1)} %copy-done.1, f32[256,128]{1,0:T(8,128)S(1)} %copy-done.2, ...), custom_call_target="tpu_custom_call" | custom-call | flops 6000000000 | bytes 12000000 | tf_op jit(solution)/shard_map/pallas_call | solution.py:335
  62.2 0.8 %copy.13 = bf16[1024,256]{1,0:T(8,128)(2,1)} copy(bf16[1024,256]{1,0:T(8,128)(2,1)S(1)} %shard_map.100) | data formatting | bytes 1048576
Async XLA Ops:
  2.5 0.7 %copy-start = (f32[1024]{0:T(1024)S(1)}, f32[1024]{0:T(1024)}, u32[]{:S(2)}) copy-start(f32[1024]{0:T(1024)} %param.12) | copy-start | bytes 12292
  3.2 1.1 %copy-start.1 = (bf16[1536,256]{1,0:T(8,128)(2,1)S(1)}, bf16[1536,256]{1,0:T(8,128)(2,1)}, u32[]{:S(2)}) copy-start(bf16[1536,256]{1,0:T(8,128)(2,1)} %constant.12.clone.small_hbm) | copy-start | bytes 2359300
  4.3 0.9 %copy-start.2 = (f32[256,128]{1,0:T(8,128)S(1)}, f32[256,128]{1,0:T(8,128)}, u32[]{:S(2)}) copy-start(f32[256,128]{1,0:T(8,128)} %constant.13.clone.twiddle_hbm) | copy-start | bytes 393220
  5.2 0.7 %copy-start.3 = (bf16[16,768]{1,0:T(8,128)(2,1)S(1)}, bf16[16,768]{1,0:T(8,128)(2,1)}, u32[]{:S(2)}) copy-start(bf16[16,768]{1,0:T(8,128)(2,1)} %constant.17.clone.edge) | copy-start | bytes 73732
  5.9 0.7 %copy-start.4 = (bf16[48,128]{1,0:T(8,128)(2,1)S(1)}, bf16[48,128]{1,0:T(8,128)(2,1)}, u32[]{:S(2)}) copy-start(bf16[48,128]{1,0:T(8,128)(2,1)} %constant.16.clone.tail) | copy-start | bytes 36868

commit v2 on v1

v2 whole, which is shorter than its diff:
```python
import functools

import jax
import jax.numpy as jnp
import ml_dtypes
import numpy as np
from jax import lax
from jax.experimental import pallas as pl
from jax.experimental.pallas import tpu as pltpu
from jax.sharding import PartitionSpec as P

MESH = pl.DeviceIdType.MESH
SIDE = 128
GROUP = 8
AHEAD = 6
f32, bf16 = jnp.float32, jnp.bfloat16


def tables(n, own, s_lo, a_lo):
    period = SIDE * SIDE
    cols = 2 * a_lo
    wide = SIDE * s_lo
    order_f = np.zeros((own * cols, own * cols))
    c, j = np.meshgrid(np.arange(own), np.arange(cols), indexing="ij")
    order_f[(c * cols + j).ravel(), (j * own + c).ravel()] = 1
    order_x = np.zeros((wide, wide))
    c, s = np.meshgrid(np.arange(SIDE), np.arange(s_lo), indexing="ij")
    order_x[(c * s_lo + s).ravel(), (s * SIDE + c).ravel()] = 1
    order_y = np.zeros((wide, wide))
    q, c, s = np.meshgrid(np.arange(SIDE // GROUP), np.arange(GROUP), np.arange(s_lo), indexing="ij")
    order_y[(s * SIDE + q * GROUP + c).ravel(), ((q * GROUP + c) * s_lo + s).ravel()] = 1
    q, part, al = (v.ravel() for v in np.meshgrid(np.arange(n), np.arange(2), np.arange(a_lo), indexing="ij"))
    angle = 2 * np.pi * ((q * a_lo + al)[:, None] * np.arange(SIDE)[None, :] % SIDE) / SIDE
    wr, wi = np.cos(angle), -np.sin(angle)
    sign = np.where(part == 1, -1.0, 1.0)[:, None]
    forward = np.concatenate([np.concatenate([wr, -wi], 1), np.concatenate([wi, wr], 1) * sign], 0)
    vr, vi = np.cos(angle).T, np.sin(angle).T
    real = (part == 0)[None, :]
    inverse = np.concatenate([np.where(real, vr, -vi), np.where(real, vi, vr)], 0)
    tail = np.zeros((3, 16, wide))
    edge = np.zeros((3, 16, 2 * SIDE))
    for e in range(3):
        tail[e, 2 * e, wide - 2] = 1
        tail[e, 2 * e + 1, wide - 1] = 1
        edge[e, 2 * e + 1, 0] = 1
        edge[e, 2 * e, SIDE] = 1
        edge[e, 2 * e + 1, SIDE + 1] = 1
    shifts = [np.eye(wide, k=by) for by in (1, 2)]
    small = np.concatenate(
        [order_f, order_x, order_y, forward, inverse, *shifts, tail.reshape(48, -1), edge.reshape(48, -1)], 0
    )
    some = GROUP // 2
    s = np.arange(n * s_lo)
    angle = 2 * np.pi * (s[:, None] * np.arange(SIDE)[None, :] % SIDE) / SIDE
    first = np.zeros((n, some, s_lo, some, 2, SIDE))
    for g in range(some):
        first[:, g, :, g, 0] = np.cos(angle).reshape(n, s_lo, SIDE)
        first[:, g, :, g, 1] = -np.sin(angle).reshape(n, s_lo, SIDE)
    first = first.reshape(n * some * s_lo, some * 2 * SIDE)
    last = first / period
    angle = 2 * np.pi * np.arange(SIDE)[:, None] * np.arange(SIDE)[None, :] / period
    twiddle = np.concatenate([np.cos(angle), np.sin(angle)], 0)
    return [
        small.astype(ml_dtypes.bfloat16),
        twiddle.astype(np.float32),
        first.astype(ml_dtypes.bfloat16),
        last.astype(ml_dtypes.bfloat16),
    ]


def peer(me, o):
    z, x, c = me // 8, (me // 2) % 4, me % 2
    return (z + o // 8) % 4 * 8 + (x + o // 2) % 4 * 2 + (c + o) % 2


def dot(a, b):
    return jnp.dot(a, b, preferred_element_type=f32)


def dot_nt(a, b):
    return lax.dot_general(a, b, (((1,), (1,)), ((), ())), preferred_element_type=f32)


def dot_tn(a, b):
    return lax.dot_general(a, b, (((0,), (0,)), ((), ())), preferred_element_type=f32)


def kernel(
    n, own, s_lo, a_lo, chunks,
    filt_hbm, proj_hbm, taps_hbm, skip_hbm, small_hbm, twiddle_hbm, first_hbm, last_hbm,
    out,
    filt, proj, taps, skip, small, twiddle, first, last,
    fsend, fbuf, xsend, xbuf, ysend, ybuf, turned, spec, values, back, conv, query, direct, halo_out, halo_in,
    load_sem, own_sem, fsend_sem, frecv_sem, xsend_sem, xrecv_sem, ysend_sem, yrecv_sem, hsend_sem, hrecv_sem,
):
    me = lax.axis_index("ctx")
    groups = own // GROUP
    cols = 2 * a_lo
    some = GROUP // 2
    xrows = GROUP * s_lo
    blocks = n * own // SIDE
    per_block = SIDE // own
    half = n * cols
    wide = SIDE * s_lo

    barrier = pltpu.get_barrier_semaphore()

    def greet(i, carry):
        pl.semaphore_signal(barrier, inc=1, device_id={"ctx": peer(me, i)}, device_id_type=MESH)
        return carry

    lax.fori_loop(1, n, greet, 0)

    loads = [
        pltpu.make_async_copy(src, dst, load_sem.at[i])
        for i, (src, dst) in enumerate(
            [(small_hbm, small), (filt_hbm, filt), (proj_hbm, proj), (taps_hbm, taps), (skip_hbm, skip), (twiddle_hbm, twiddle), (first_hbm, first), (last_hbm, last)]
        )
    ]
    for load in loads:
        load.start()

    order_f = small.at[pl.ds(0, 256)]
    order_x = small.at[pl.ds(256, 256)]
    order_y = small.at[pl.ds(512, 256)]
    forward = small.at[pl.ds(768, 512)]
    inverse = small.at[pl.ds(1280, 256)]
    shifts = [small.at[pl.ds(1536, 256)], small.at[pl.ds(1792, 256)]]
    tails = [small.at[pl.ds(2048 + 16 * e, 16)] for e in range(3)]
    edges = [small.at[pl.ds(2096 + 16 * e, 16)] for e in range(3)]

    def at_peer(i):
        return peer(me, i * 11 % n)

    def arrange(i):
        owners = at_peer(2 * i), at_peer(2 * i + 1)
        sides = []
        for d in owners:
            rows = pl.ds(pl.multiple_of(d * own, own), own)
            sides.append([filt[part, rows, al * SIDE : (al + 1) * SIDE] for part in range(2) for al in range(a_lo)])
        stacked = jnp.concatenate([jnp.concatenate(side, axis=0) for side in sides], axis=1)
        arranged = dot(order_f[...], stacked).astype(bf16)
        for k, d in enumerate(owners):
            fsend[d] = arranged[:, k * SIDE : (k + 1) * SIDE]

    def f_rows(chunk):
        start, count = chunks[chunk]
        return pl.ds(start * 2 * cols, count * 2 * cols)

    def f_send(chunk, i):
        rows = f_rows(chunk)
        d = at_peer(i)
        pltpu.make_async_remote_copy(
            src_ref=fsend.at[d, rows], dst_ref=fbuf.at[me, rows], send_sem=fsend_sem.at[chunk], recv_sem=frecv_sem.at[chunk],
            device_id={"ctx": d}, device_id_type=MESH,
        ).start()

    def f_all(chunk):
        rows = f_rows(chunk)
        return pltpu.make_async_remote_copy(
            src_ref=fsend.at[pl.ds(0, n - 1), rows], dst_ref=fbuf.at[pl.ds(0, n - 1), rows],
            send_sem=fsend_sem.at[chunk], recv_sem=frecv_sem.at[chunk],
            device_id={"ctx": (me + 1) % n}, device_id_type=MESH,
        )

    loads[0].wait()
    loads[1].wait()

    def ahead(i, carry):
        arrange(i)
        return carry

    lax.fori_loop(0, AHEAD, ahead, 0)
    own_f = pltpu.make_async_copy(fsend.at[me], fbuf.at[me], own_sem.at[0])
    own_f.start()

    loads[2].wait()
    halo_out[...] = sum(dot_nt(tails[e][...], proj[e]) for e in range(3)).astype(bf16)

    pl.semaphore_wait(barrier, n - 1)

    halo = pltpu.make_async_remote_copy(
        src_ref=halo_out, dst_ref=halo_in, send_sem=hsend_sem, recv_sem=hrecv_sem,
        device_id={"ctx": (me + 1) % n}, device_id_type=MESH,
    )
    halo.start()

    def send_ready(i, carry):
        f_send(0, i)
        return carry

    lax.fori_loop(1, 2 * AHEAD, send_ready, 0)

    def arrange_send(i, carry):
        arrange(i)
        f_send(0, 2 * i)
        f_send(0, 2 * i + 1)
        return carry

    lax.fori_loop(AHEAD, n // 2, arrange_send, 0)

    loads[3].wait()
    loads[4].wait()
    halo.wait_recv()
    inside = jnp.where(me == 0, 0.0, 1.0).astype(f32)

    def gate(blk, carry):
        rows = pl.ds(pl.multiple_of(blk * SIDE, SIDE), SIDE)
        halo_rows = halo_in[:, rows]
        columns = jnp.concatenate(
            [taps[e, :, rows] for e in range(3)] + [skip[pl.ds(blk, 1), :], jnp.zeros((SIDE - 10, SIDE), f32)], axis=0
        ).T
        filtered = []
        for e in range(3):
            x = proj[e, rows, :]
            before = dot_tn(halo_rows, edges[e][...]) * inside
            back1, back2 = dot(x, shifts[0][...]), dot(x, shifts[1][...])
            back1 = jnp.concatenate([back1[:, :SIDE] + before[:, :SIDE], back1[:, SIDE:]], axis=1)
            back2 = jnp.concatenate([back2[:, :SIDE] + before[:, SIDE:], back2[:, SIDE:]], axis=1)
            tap = columns[:, 3 * e : 3 * e + 3]
            filtered.append(tap[:, 0:1] * x.astype(f32) + tap[:, 1:2] * back1 + tap[:, 2:3] * back2)
        product = (filtered[1] * filtered[2]).astype(bf16)
        owners = pl.ds(pl.multiple_of(blk * per_block, per_block), per_block)
        query[owners] = filtered[0].reshape(per_block, own, wide)
        direct[owners] = (columns[:, 9:10] * product.astype(f32)).reshape(per_block, own, wide)
        stacked = jnp.concatenate([product[:, s * SIDE : (s + 1) * SIDE] for s in range(s_lo)], axis=0)
        xsend[owners] = dot(order_x[...], stacked).astype(bf16).reshape(per_block, own * s_lo, SIDE)
        return carry

    lax.fori_loop(0, blocks, gate, 0)

    x_all = pltpu.make_async_remote_copy(
        src_ref=xsend.at[pl.ds(0, n - 1)], dst_ref=xbuf.at[pl.ds(0, n - 1)], send_sem=xsend_sem, recv_sem=xrecv_sem,
        device_id={"ctx": (me + 1) % n}, device_id_type=MESH,
    )

    def x_start(i, carry):
        d = at_peer(i)
        pltpu.make_async_remote_copy(
            src_ref=xsend.at[d], dst_ref=xbuf.at[me], send_sem=xsend_sem, recv_sem=xrecv_sem,
            device_id={"ctx": d}, device_id_type=MESH,
        ).start()
        return carry

    lax.fori_loop(1, n, x_start, 0)
    own_x = pltpu.make_async_copy(xsend.at[me], xbuf.at[me], own_sem.at[1])
    own_x.start()

    for chunk in range(1, len(chunks)):

        def f_start(i, carry, chunk=chunk):
            f_send(chunk, i)
            return carry

        lax.fori_loop(1, n, f_start, 0)

    for load in loads[5:]:
        load.wait()
    own_x.wait()
    x_all.wait_recv()
    cos, sin = twiddle[0:SIDE, :], twiddle[SIDE : 2 * SIDE, :]

    for g in range(groups):
        taken = xbuf[:, g * xrows : (g + 1) * xrows, :].astype(f32)
        for k in range(2):
            block = taken[:, k * some * s_lo : (k + 1) * some * s_lo, :].reshape(n * some * s_lo, SIDE)
            turned[(2 * g + k) * SIDE : (2 * g + k + 1) * SIDE, :] = block.T.astype(bf16)

    def over_s(g, carry):
        rows = pl.ds(pl.multiple_of(g * 2 * SIDE, 2 * SIDE), 2 * SIDE)
        for c in range(some):
            part = dot(turned[rows, :], first[:, c * 2 * SIDE : (c + 1) * 2 * SIDE])
            lanes = slice(c % 2 * SIDE, (c % 2 + 1) * SIDE)
            for k in range(2):
                re, im = part[k * SIDE : (k + 1) * SIDE, :SIDE], part[k * SIDE : (k + 1) * SIDE, SIDE:]
                pair = g * some + k * 2 + c // 2
                spec[pair, 0:SIDE, lanes] = (re * cos + im * sin).astype(bf16)
                spec[pair, SIDE : 2 * SIDE, lanes] = (im * cos - re * sin).astype(bf16)
        return carry

    lax.fori_loop(0, groups, over_s, 0)

    def over_r(i, carry):
        for k in range(2):
            values[2 * i + k] = dot(forward[...], spec[2 * i + k])
        return carry

    lax.fori_loop(0, own // 4, over_r, 0)

    own_f.wait()

    def through(h, k):
        for j in range(2):
            pair = 2 * h + j
            taken = fbuf[:, pl.ds(pl.multiple_of(pair * 2 * cols, 2 * cols), 2 * cols), :].astype(f32)
            shaped = []
            for c in range(2):
                gains = taken[:, c * cols : (c + 1) * cols, :]
                lanes = slice(c * SIDE, (c + 1) * SIDE)
                straight = values[pair, 0:half, lanes].reshape(n, cols, SIDE) * gains
                crossed = values[pair, half : 2 * half, lanes].reshape(n, cols, SIDE) * gains
                shaped.append((straight + pltpu.roll(crossed, a_lo, 1)).reshape(half, SIDE).astype(bf16))
            part = dot(inverse[...], jnp.concatenate(shaped, axis=1))
            rows = pl.ds(pl.multiple_of(k * SIDE, SIDE), SIDE)
            for c in range(2):
                re, im = part[:SIDE, c * SIDE : (c + 1) * SIDE], part[SIDE:, c * SIDE : (c + 1) * SIDE]
                at = (2 * j + c) * 2 * SIDE
                back[rows, at : at + SIDE] = (re * cos - im * sin).astype(bf16)
                back[rows, at + SIDE : at + 2 * SIDE] = (re * sin + im * cos).astype(bf16)

    def y_all(g):
        return pltpu.make_async_remote_copy(
            src_ref=ysend.at[g, pl.ds(0, (n - 1) * xrows)], dst_ref=ybuf.at[g, pl.ds(0, (n - 1) * xrows)],
            send_sem=ysend_sem.at[g], recv_sem=yrecv_sem.at[g], device_id={"ctx": (me + 1) % n}, device_id_type=MESH,
        )

    arrives = {start: chunk for chunk, (start, _) in enumerate(chunks)}
    own_y = []
    for g in range(groups):
        pairs = range(some * g, some * g + some)
        if pairs[0] in arrives:
            f_all(arrives[pairs[0]]).wait_recv()
        if pairs[2] in arrives:
            through(2 * g, 0)
            f_all(arrives[pairs[2]]).wait_recv()
            through(2 * g + 1, 1)
        else:

            def both(k, carry, g=g):
                through(2 * g + k, k)
                return carry

            lax.fori_loop(0, 2, both, 0)
        part = dot_nt(last[...], back[...])
        part = jnp.concatenate([part[:, k * SIDE : (k + 1) * SIDE].reshape(n, some * s_lo, SIDE) for k in range(2)], axis=1)
        ysend[g] = part.reshape(n * xrows, SIDE).astype(bf16)

        def y_start(i, carry, g=g):
            d = at_peer(i)
            pltpu.make_async_remote_copy(
                src_ref=ysend.at[g, pl.ds(pl.multiple_of(d * xrows, xrows), xrows)],
                dst_ref=ybuf.at[g, pl.ds(pl.multiple_of(me * xrows, xrows), xrows)],
                send_sem=ysend_sem.at[g], recv_sem=yrecv_sem.at[g], device_id={"ctx": d}, device_id_type=MESH,
            ).start()
            return carry

        lax.fori_loop(1, n, y_start, 0)
        mine = pl.ds(pl.multiple_of(me * xrows, xrows), xrows)
        own_y.append(pltpu.make_async_copy(ysend.at[g, mine], ybuf.at[g, mine], own_sem.at[2 + g]))
        own_y[g].start()

    owners = SIDE // GROUP
    for g in range(groups):
        own_y[g].wait()
        y_all(g).wait_recv()
        count = n // owners
        stacked = [ybuf[g, h * owners * xrows : (h + 1) * owners * xrows, :] for h in range(count)]
        arranged = dot(order_y[...], jnp.concatenate(stacked, axis=1))
        for h in range(count):
            for s in range(s_lo):
                conv[h * owners : (h + 1) * owners, g * GROUP : (g + 1) * GROUP, s * SIDE : (s + 1) * SIDE] = arranged[
                    s * SIDE : (s + 1) * SIDE, h * SIDE : (h + 1) * SIDE
                ].reshape(owners, GROUP, SIDE)
        if g % 2 == 1:
            rows = slice((g - 1) * GROUP, (g + 1) * GROUP)
            out[:, rows, :] = (query[:, rows, :] * (conv[:, rows, :] + direct[:, rows, :])).astype(bf16)

    halo.wait_send()
    x_all.wait_send()
    for chunk in range(len(chunks)):
        f_all(chunk).wait_send()
    for g in range(groups):
        y_all(g).wait_send()


def shards(projections, short_filter, skip_gain, filter_spectra):
    n = lax.axis_size("ctx")
    channels, tokens = projections.shape[1:]
    freqs = filter_spectra.shape[2]
    own, s_lo, a_lo = channels // n, tokens // SIDE, freqs // SIDE
    groups = own // GROUP
    cols = 2 * a_lo
    pairs = own // 2
    chunks = [(0, pairs // 2), (pairs // 2, pairs // 4), (pairs * 3 // 4, pairs // 8), (pairs * 7 // 8, pairs // 8)]
    hbm, vmem = pl.BlockSpec(memory_space=pltpu.HBM), pl.BlockSpec(memory_space=pltpu.VMEM)
    small, twiddle, first, last = tables(n, own, s_lo, a_lo)
    dma = pltpu.SemaphoreType.DMA
    return pl.pallas_call(
        functools.partial(kernel, n, own, s_lo, a_lo, chunks),
        out_shape=jax.ShapeDtypeStruct((n, own, tokens), bf16),
        in_specs=[hbm] * 8,
        out_specs=vmem,
        scratch_shapes=[
            pltpu.VMEM(filter_spectra.shape, bf16),
            pltpu.VMEM(projections.shape, bf16),
            pltpu.VMEM((3, 3, channels), f32),
            pltpu.VMEM((channels // SIDE, SIDE), f32),
            pltpu.VMEM(small.shape, bf16),
            pltpu.VMEM(twiddle.shape, f32),
            pltpu.VMEM(first.shape, bf16),
            pltpu.VMEM(last.shape, bf16),
            pltpu.VMEM((n, own * cols, SIDE), bf16),
            pltpu.VMEM((n, own * cols, SIDE), bf16),
            pltpu.VMEM((n, own * s_lo, SIDE), bf16),
            pltpu.VMEM((n, own * s_lo, SIDE), bf16),
            pltpu.VMEM((groups, n * GROUP * s_lo, SIDE), bf16),
            pltpu.VMEM((groups, n * GROUP * s_lo, SIDE), bf16),
            pltpu.VMEM((2 * groups * SIDE, n * GROUP * s_lo // 2), bf16),
            pltpu.VMEM((own // 2, 2 * SIDE, 2 * SIDE), bf16),
            pltpu.VMEM((own // 2, 4 * SIDE, 2 * SIDE), f32),
            pltpu.VMEM((2 * SIDE, GROUP * SIDE), bf16),
            pltpu.VMEM((n, own, tokens), f32),
            pltpu.VMEM((n, own, tokens), f32),
            pltpu.VMEM((n, own, tokens), f32),
            pltpu.VMEM((16, channels), bf16),
            pltpu.VMEM((16, channels), bf16),
            dma((8,)),
            dma((2 + groups,)),
            dma((len(chunks),)),
            dma((len(chunks),)),
            dma,
            dma,
            dma((groups,)),
            dma((groups,)),
            dma,
            dma,
        ],
        compiler_params=pltpu.CompilerParams(collective_id=0, has_side_effects=True, vmem_limit_bytes=62 << 20),
        cost_estimate=pl.CostEstimate(flops=6_000_000_000, bytes_accessed=12_000_000, transcendentals=0),
    )(
        filter_spectra, projections, jnp.swapaxes(short_filter, 1, 2), skip_gain.reshape(channels // SIDE, SIDE),
        small, twiddle, first, last,
    ).reshape(channels, tokens)


def solution(mesh):
    return jax.shard_map(
        shards,
        mesh=mesh,
        in_specs=(P(None, "ch", "ctx"), P(None, "ch", None), P("ch"), P(None, "ch", "ctx")),
        out_specs=P("ch", "ctx"),
        check_vma=False,
    )
```

time: 63.4 us -> 51.1 us (0.81)
  Pallas kernels: 55.6 us -> 49.1 us
  local copies, waits for them, and re-layouts: 7.43 us -> 1.87 us
    pallas_call x1, Pallas kernels: 55.6 us -> 49.1 us  [shards(): pl.pallas_call(functools.partial(kernel, n, own, s_lo, a_lo, chunks), out...]
    unnamed x12 -> x1, local copies, waits for them, and re-layouts: 7.43 us -> 1.87 us
where the time goes in v2:
time: 51.1 us; the launch traced here: 50.9 us
  Pallas kernels  49.1 us (96%)
  local copies, waits for them, and re-layouts  1.87 us (4%)
    pallas_call x1, Pallas kernels, shards(): pl.pallas_call(functools.partial(kernel, n, own, s_lo, a_lo, chunks), out...  49.1 us
    unnamed x1, local copies, waits for them, and re-layouts  1.87 us

profile of v2, /device:TPU:1, one launch (start us, length us, event | category | flops | bytes accessed | tf_op | source)
XLA Modules:
  0.0 50.9 jit_solution(1932003654294706515)
XLA Ops:
  0.0 49.1 %shard_map.82 = bf16[32,32,256]{2,1,0:T(8,128)(2,1)} custom-call(bf16[2,1024,512]{2,1,0:T(8,128)(2,1)} %filt_hbm.1, bf16[3,1024,256]{2,1,0:T(8,128)(2,1)} %proj_hbm.1, f32[3,3,1024]{2,1,0:T(4,128)} %bitcast.4, f32[8,128]{1,0:T(8,128)} %bitcast.5, bf16[2144,256]{1,0:T(8,128)(2,1)} %constant.8.clone.small_hbm, f32[256,128]{1,0:T(8,128)} %constant.9.clone.twiddle_hbm, ...), custom_call_target="tpu_custom_call" | custom-call | flops 6000000000 | bytes 12000000 | tf_op jit(solution)/shard_map/pallas_call | solution.py:388
  49.1 1.9 %copy.10 = bf16[1024,256]{1,0:T(8,128)(2,1)} copy(bf16[1024,256]{1,0:T(8,128)(2,1)} %bitcast.3) | data formatting | bytes 1048576

commit v3 on v2

--- a/solution.py
+++ b/solution.py
@@ -68,11 +68,6 @@
     ]
 
 
-def peer(me, o):
-    z, x, c = me // 8, (me // 2) % 4, me % 2
-    return (z + o // 8) % 4 * 8 + (x + o // 2) % 4 * 2 + (c + o) % 2
-
-
 def dot(a, b):
     return jnp.dot(a, b, preferred_element_type=f32)
 
@@ -106,10 +101,10 @@
     barrier = pltpu.get_barrier_semaphore()
 
     def greet(i, carry):
-        pl.semaphore_signal(barrier, inc=1, device_id={"ctx": peer(me, i)}, device_id_type=MESH)
-        return carry
-
-    lax.fori_loop(1, n, greet, 0)
+        pl.semaphore_signal(barrier, inc=1, device_id={"ctx": lax.rem(me + i, n)}, device_id_type=MESH)
+        return carry
+
+    lax.fori_loop(1, n, greet, 0, unroll=True)
 
     loads = [
         pltpu.make_async_copy(src, dst, load_sem.at[i])
@@ -130,7 +125,7 @@
     edges = [small.at[pl.ds(2096 + 16 * e, 16)] for e in range(3)]
 
     def at_peer(i):
-        return peer(me, i * 11 % n)
+        return lax.rem(me + i * 5, n)
 
     def arrange(i):
         owners = at_peer(2 * i), at_peer(2 * i + 1)

time: 51.1 us -> 49 us (0.959)
  Pallas kernels: 49.1 us -> 46.9 us
    pallas_call x1, Pallas kernels: 49.1 us -> 46.9 us  [shards(): pl.pallas_call(functools.partial(kernel, n, own, s_lo, a_lo, chunks), out...]
where the time goes in v3:
time: 49 us; the launch traced here: 48.8 us
  Pallas kernels  46.9 us (96%)
  local copies, waits for them, and re-layouts  1.87 us (4%)
    pallas_call x1, Pallas kernels, shards(): pl.pallas_call(functools.partial(kernel, n, own, s_lo, a_lo, chunks), out...  46.9 us
    unnamed x1, local copies, waits for them, and re-layouts  1.87 us

profile of v3, /device:TPU:1, one launch (start us, length us, event | category | flops | bytes accessed | tf_op | source)
XLA Modules:
  0.0 48.8 jit_solution(16146304122601565406)
XLA Ops:
  0.0 46.9 %shard_map.82 = bf16[32,32,256]{2,1,0:T(8,128)(2,1)} custom-call(bf16[2,1024,512]{2,1,0:T(8,128)(2,1)} %filt_hbm.1, bf16[3,1024,256]{2,1,0:T(8,128)(2,1)} %proj_hbm.1, f32[3,3,1024]{2,1,0:T(4,128)} %bitcast.4, f32[8,128]{1,0:T(8,128)} %bitcast.5, bf16[2144,256]{1,0:T(8,128)(2,1)} %constant.8.clone.small_hbm, f32[256,128]{1,0:T(8,128)} %constant.9.clone.twiddle_hbm, ...), custom_call_target="tpu_custom_call" | custom-call | flops 6000000000 | bytes 12000000 | tf_op jit(solution)/shard_map/pallas_call | solution.py:383
  47.0 1.9 %copy.10 = bf16[1024,256]{1,0:T(8,128)(2,1)} copy(bf16[1024,256]{1,0:T(8,128)(2,1)} %bitcast.3) | data formatting | bytes 1048576

commit v4 on v3

--- a/solution.py
+++ b/solution.py
@@ -380,6 +380,10 @@
     hbm, vmem = pl.BlockSpec(memory_space=pltpu.HBM), pl.BlockSpec(memory_space=pltpu.VMEM)
     small, twiddle, first, last = tables(n, own, s_lo, a_lo)
     dma = pltpu.SemaphoreType.DMA
+    operands = [
+        filter_spectra, projections, jnp.swapaxes(short_filter, 1, 2), skip_gain.reshape(channels // SIDE, SIDE),
+        *(jnp.asarray(table) for table in (small, twiddle, first, last)),
+    ]
     return pl.pallas_call(
         functools.partial(kernel, n, own, s_lo, a_lo, chunks),
         out_shape=jax.ShapeDtypeStruct((n, own, tokens), bf16),
@@ -420,12 +424,9 @@
             dma,
             dma,
         ],
-        compiler_params=pltpu.CompilerParams(collective_id=0, has_side_effects=True, vmem_limit_bytes=62 << 20),
+        compiler_params=pltpu.CompilerParams(collective_id=0, has_side_effects=True, vmem_limit_bytes=52 << 20),
         cost_estimate=pl.CostEstimate(flops=6_000_000_000, bytes_accessed=12_000_000, transcendentals=0),
-    )(
-        filter_spectra, projections, jnp.swapaxes(short_filter, 1, 2), skip_gain.reshape(channels // SIDE, SIDE),
-        small, twiddle, first, last,
-    ).reshape(channels, tokens)
+    )(*(pltpu.with_memory_space_constraint(x, pltpu.HBM) for x in operands)).reshape(channels, tokens)
 
 
 def solution(mesh):

time: 49 us -> 47.1 us (0.961)
  local copies, waits for them, and re-layouts: 1.87 us -> 0.8 us
  Pallas kernels: 46.9 us -> 46.1 us
    unnamed x1, local copies, waits for them, and re-layouts: 1.87 us -> 0.8 us
    pallas_call x1, Pallas kernels: 46.9 us -> 46.1 us  [shards(): pl.pallas_call(functools.partial(kernel, n, own, s_lo, a_lo, chunks), out...]
where the time goes in v4:
time: 47.1 us; the launch traced here: 47 us
  Pallas kernels  46.1 us (98%)
  local copies, waits for them, and re-layouts  0.8 us (2%)
    pallas_call x1, Pallas kernels, shards(): pl.pallas_call(functools.partial(kernel, n, own, s_lo, a_lo, chunks), out...  46.1 us

profile of v4, /device:TPU:1, one launch (start us, length us, event | category | flops | bytes accessed | tf_op | source)
XLA Modules:
  0.0 47.0 jit_solution(15310469851822659496)
XLA Ops:
  0.0 46.1 %shard_map.82 = bf16[32,32,256]{2,1,0:T(8,128)(2,1)S(1)} custom-call(bf16[2,1024,512]{2,1,0:T(8,128)(2,1)} %filt_hbm.1, bf16[3,1024,256]{2,1,0:T(8,128)(2,1)} %proj_hbm.1, f32[3,3,1024]{2,1,0:T(4,128)} %bitcast.4, f32[8,128]{1,0:T(8,128)} %bitcast.5, bf16[2144,256]{1,0:T(8,128)(2,1)} %constant.8.clone.small_hbm, f32[256,128]{1,0:T(8,128)} %constant.9.clone.twiddle_hbm, ...), custom_call_target="tpu_custom_call" | custom-call | flops 6000000000 | bytes 12000000 | tf_op jit(solution)/shard_map/pallas_call | solution.py:387
  46.2 0.8 %copy.10 = bf16[1024,256]{1,0:T(8,128)(2,1)} copy(bf16[1024,256]{1,0:T(8,128)(2,1)S(1)} %bitcast.3) | data formatting | bytes 1048576

commit v5 on v4

--- a/solution.py
+++ b/solution.py
@@ -12,7 +12,7 @@
 MESH = pl.DeviceIdType.MESH
 SIDE = 128
 GROUP = 8
-AHEAD = 6
+AHEAD = 3
 f32, bf16 = jnp.float32, jnp.bfloat16
 
 
@@ -81,7 +81,7 @@
 
 
 def kernel(
-    n, own, s_lo, a_lo, chunks,
+    n, own, s_lo, a_lo, chunks, returns,
     filt_hbm, proj_hbm, taps_hbm, skip_hbm, small_hbm, twiddle_hbm, first_hbm, last_hbm,
     out,
     filt, proj, taps, skip, small, twiddle, first, last,
@@ -106,14 +106,18 @@
 
     lax.fori_loop(1, n, greet, 0, unroll=True)
 
-    loads = [
+    head, rest = pl.ds(0, 256), pl.ds(256, small.shape[0] - 256)
+    load_head, load_filt, load_proj, load_rest, load_taps, load_skip, *load_late = [
         pltpu.make_async_copy(src, dst, load_sem.at[i])
         for i, (src, dst) in enumerate(
-            [(small_hbm, small), (filt_hbm, filt), (proj_hbm, proj), (taps_hbm, taps), (skip_hbm, skip), (twiddle_hbm, twiddle), (first_hbm, first), (last_hbm, last)]
+            [
+                (small_hbm.at[head], small.at[head]), (filt_hbm, filt), (proj_hbm, proj), (small_hbm.at[rest], small.at[rest]),
+                (taps_hbm, taps), (skip_hbm, skip), (twiddle_hbm, twiddle), (first_hbm, first), (last_hbm, last),
+            ]
         )
     ]
-    for load in loads:
-        load.start()
+    load_head.start()
+    load_filt.start()
 
     order_f = small.at[pl.ds(0, 256)]
     order_x = small.at[pl.ds(256, 256)]
@@ -158,8 +162,10 @@
             device_id={"ctx": (me + 1) % n}, device_id_type=MESH,
         )
 
-    loads[0].wait()
-    loads[1].wait()
+    load_head.wait()
+    load_filt.wait()
+    for load in (load_proj, load_rest, load_taps, load_skip, *load_late):
+        load.start()
 
     def ahead(i, carry):
         arrange(i)
@@ -169,23 +175,23 @@
     own_f = pltpu.make_async_copy(fsend.at[me], fbuf.at[me], own_sem.at[0])
     own_f.start()
 
-    loads[2].wait()
+    pl.semaphore_wait(barrier, n - 1)
+
+    def send_ready(i, carry):
+        f_send(0, i)
+        return carry
+
+    lax.fori_loop(1, 2 * AHEAD, send_ready, 0)
+
+    load_proj.wait()
+    load_rest.wait()
     halo_out[...] = sum(dot_nt(tails[e][...], proj[e]) for e in range(3)).astype(bf16)
-
-    pl.semaphore_wait(barrier, n - 1)
-
     halo = pltpu.make_async_remote_copy(
         src_ref=halo_out, dst_ref=halo_in, send_sem=hsend_sem, recv_sem=hrecv_sem,
         device_id={"ctx": (me + 1) % n}, device_id_type=MESH,
     )
     halo.start()
 
-    def send_ready(i, carry):
-        f_send(0, i)
-        return carry
-
-    lax.fori_loop(1, 2 * AHEAD, send_ready, 0)
-
     def arrange_send(i, carry):
         arrange(i)
         f_send(0, 2 * i)
@@ -194,8 +200,8 @@
 
     lax.fori_loop(AHEAD, n // 2, arrange_send, 0)
 
-    loads[3].wait()
-    loads[4].wait()
+    load_taps.wait()
+    load_skip.wait()
     halo.wait_recv()
     inside = jnp.where(me == 0, 0.0, 1.0).astype(f32)
 
@@ -249,7 +255,7 @@
 
         lax.fori_loop(1, n, f_start, 0)
 
-    for load in loads[5:]:
+    for load in load_late:
         load.wait()
     own_x.wait()
     x_all.wait_recv()
@@ -303,12 +309,17 @@
                 back[rows, at : at + SIDE] = (re * cos - im * sin).astype(bf16)
                 back[rows, at + SIDE : at + 2 * SIDE] = (re * sin + im * cos).astype(bf16)
 
-    def y_all(g):
+    def y_copy(k, src, dst, d):
+        rows = pl.ds(returns[k][0] * xrows, returns[k][1] * xrows)
         return pltpu.make_async_remote_copy(
-            src_ref=ysend.at[g, pl.ds(0, (n - 1) * xrows)], dst_ref=ybuf.at[g, pl.ds(0, (n - 1) * xrows)],
-            send_sem=ysend_sem.at[g], recv_sem=yrecv_sem.at[g], device_id={"ctx": (me + 1) % n}, device_id_type=MESH,
+            src_ref=ysend.at[src, rows], dst_ref=ybuf.at[dst, rows], send_sem=ysend_sem.at[k], recv_sem=yrecv_sem.at[k],
+            device_id={"ctx": d}, device_id_type=MESH,
         )
 
+    def y_all(k):
+        return y_copy(k, pl.ds(0, n - 1), pl.ds(0, n - 1), (me + 1) % n)
+
+    sends = {start + count - 1: k for k, (start, count) in enumerate(returns)}
     arrives = {start: chunk for chunk, (start, _) in enumerate(chunks)}
     own_y = []
     for g in range(groups):
@@ -317,8 +328,10 @@
             f_all(arrives[pairs[0]]).wait_recv()
         if pairs[2] in arrives:
             through(2 * g, 0)
+            early = dot_nt(last[...], back[0:SIDE, :])
             f_all(arrives[pairs[2]]).wait_recv()
             through(2 * g + 1, 1)
+            parts = [early, dot_nt(last[...], back[SIDE : 2 * SIDE, :])]
         else:
 
             def both(k, carry, g=g):
@@ -326,30 +339,34 @@
                 return carry
 
             lax.fori_loop(0, 2, both, 0)
-        part = dot_nt(last[...], back[...])
-        part = jnp.concatenate([part[:, k * SIDE : (k + 1) * SIDE].reshape(n, some * s_lo, SIDE) for k in range(2)], axis=1)
-        ysend[g] = part.reshape(n * xrows, SIDE).astype(bf16)
-
-        def y_start(i, carry, g=g):
+            part = dot_nt(last[...], back[...])
+            parts = [part[:, k * SIDE : (k + 1) * SIDE] for k in range(2)]
+        part = jnp.concatenate([part.reshape(n, some * s_lo, SIDE) for part in parts], axis=1)
+        ysend[:, g * xrows : (g + 1) * xrows, :] = part.astype(bf16)
+        if g not in sends:
+            continue
+
+        def y_start(i, carry, k=sends[g]):
             d = at_peer(i)
-            pltpu.make_async_remote_copy(
-                src_ref=ysend.at[g, pl.ds(pl.multiple_of(d * xrows, xrows), xrows)],
-                dst_ref=ybuf.at[g, pl.ds(pl.multiple_of(me * xrows, xrows), xrows)],
-                send_sem=ysend_sem.at[g], recv_sem=yrecv_sem.at[g], device_id={"ctx": d}, device_id_type=MESH,
-            ).start()
+            y_copy(k, d, me, d).start()
             return carry
 
         lax.fori_loop(1, n, y_start, 0)
-        mine = pl.ds(pl.multiple_of(me * xrows, xrows), xrows)
-        own_y.append(pltpu.make_async_copy(ysend.at[g, mine], ybuf.at[g, mine], own_sem.at[2 + g]))
-        own_y[g].start()
+        start, count = returns[sends[g]]
+        mine = pl.ds(start * xrows, count * xrows)
+        own_y.append(pltpu.make_async_copy(ysend.at[me, mine], ybuf.at[me, mine], own_sem.at[2 + sends[g]]))
+        own_y[-1].start()
 
     owners = SIDE // GROUP
     for g in range(groups):
-        own_y[g].wait()
-        y_all(g).wait_recv()
+        for k, (start, _) in enumerate(returns):
+            if g == start:
+                own_y[k].wait()
+                y_all(k).wait_recv()
         count = n // owners
-        stacked = [ybuf[g, h * owners * xrows : (h + 1) * owners * xrows, :] for h in range(count)]
+        stacked = [
+            ybuf[h * owners : (h + 1) * owners, g * xrows : (g + 1) * xrows, :].reshape(owners * xrows, SIDE) for h in range(count)
+        ]
         arranged = dot(order_y[...], jnp.concatenate(stacked, axis=1))
         for h in range(count):
             for s in range(s_lo):
@@ -364,8 +381,8 @@
     x_all.wait_send()
     for chunk in range(len(chunks)):
         f_all(chunk).wait_send()
-    for g in range(groups):
-        y_all(g).wait_send()
+    for k in range(len(returns)):
+        y_all(k).wait_send()
 
 
 def shards(projections, short_filter, skip_gain, filter_spectra):
@@ -377,6 +394,7 @@
     cols = 2 * a_lo
     pairs = own // 2
     chunks = [(0, pairs // 2), (pairs // 2, pairs // 4), (pairs * 3 // 4, pairs // 8), (pairs * 7 // 8, pairs // 8)]
+    returns = [(0, groups * 3 // 4), (groups * 3 // 4, groups // 4)]
     hbm, vmem = pl.BlockSpec(memory_space=pltpu.HBM), pl.BlockSpec(memory_space=pltpu.VMEM)
     small, twiddle, first, last = tables(n, own, s_lo, a_lo)
     dma = pltpu.SemaphoreType.DMA
@@ -385,7 +403,7 @@
         *(jnp.asarray(table) for table in (small, twiddle, first, last)),
     ]
     return pl.pallas_call(
-        functools.partial(kernel, n, own, s_lo, a_lo, chunks),
+        functools.partial(kernel, n, own, s_lo, a_lo, chunks, returns),
         out_shape=jax.ShapeDtypeStruct((n, own, tokens), bf16),
         in_specs=[hbm] * 8,
         out_specs=vmem,
@@ -402,8 +420,8 @@
             pltpu.VMEM((n, own * cols, SIDE), bf16),
             pltpu.VMEM((n, own * s_lo, SIDE), bf16),
             pltpu.VMEM((n, own * s_lo, SIDE), bf16),
-            pltpu.VMEM((groups, n * GROUP * s_lo, SIDE), bf16),
-            pltpu.VMEM((groups, n * GROUP * s_lo, SIDE), bf16),
+            pltpu.VMEM((n, own * s_lo, SIDE), bf16),
+            pltpu.VMEM((n, own * s_lo, SIDE), bf16),
             pltpu.VMEM((2 * groups * SIDE, n * GROUP * s_lo // 2), bf16),
             pltpu.VMEM((own // 2, 2 * SIDE, 2 * SIDE), bf16),
             pltpu.VMEM((own // 2, 4 * SIDE, 2 * SIDE), f32),
@@ -413,14 +431,14 @@
             pltpu.VMEM((n, own, tokens), f32),
             pltpu.VMEM((16, channels), bf16),
             pltpu.VMEM((16, channels), bf16),
-            dma((8,)),
-            dma((2 + groups,)),
+            dma((9,)),
+            dma((2 + len(returns),)),
             dma((len(chunks),)),
             dma((len(chunks),)),
             dma,
             dma,
-            dma((groups,)),
-            dma((groups,)),
+            dma((len(returns),)),
+            dma((len(returns),)),
             dma,
             dma,
         ],

time: 47.1 us -> 46.8 us (level)
  no operation moved by 1% of the time
where the time goes in v5:
time: 46.8 us; the launch traced here: 46.6 us
  Pallas kernels  45.8 us (98%)
  local copies, waits for them, and re-layouts  0.8 us (2%)
    pallas_call x1, Pallas kernels, shards(): pl.pallas_call(functools.partial(kernel, n, own, s_lo, a_lo, chunks, retu...  45.8 us

profile of v5, /device:TPU:1, one launch (start us, length us, event | category | flops | bytes accessed | tf_op | source)
XLA Modules:
  0.0 46.6 jit_solution(4938452029160442519)
XLA Ops:
  0.0 45.8 %shard_map.82 = bf16[32,32,256]{2,1,0:T(8,128)(2,1)S(1)} custom-call(bf16[2,1024,512]{2,1,0:T(8,128)(2,1)} %filt_hbm.1, bf16[3,1024,256]{2,1,0:T(8,128)(2,1)} %proj_hbm.1, f32[3,3,1024]{2,1,0:T(4,128)} %bitcast.4, f32[8,128]{1,0:T(8,128)} %bitcast.5, bf16[2144,256]{1,0:T(8,128)(2,1)} %constant.8.clone.small_hbm, f32[256,128]{1,0:T(8,128)} %constant.9.clone.twiddle_hbm, ...), custom_call_target="tpu_custom_call" | custom-call | flops 6000000000 | bytes 12000000 | tf_op jit(solution)/shard_map/pallas_call | solution.py:405
  45.8 0.8 %copy.10 = bf16[1024,256]{1,0:T(8,128)(2,1)} copy(bf16[1024,256]{1,0:T(8,128)(2,1)S(1)} %bitcast.3) | data formatting | bytes 1048576

commit v6 on v5

--- a/solution.py
+++ b/solution.py
@@ -286,7 +286,7 @@
             values[2 * i + k] = dot(forward[...], spec[2 * i + k])
         return carry
 
-    lax.fori_loop(0, own // 4, over_r, 0)
+    lax.fori_loop(0, own // 4, over_r, 0, unroll=2)
 
     own_f.wait()
 
@@ -338,7 +338,7 @@
                 through(2 * g + k, k)
                 return carry
 
-            lax.fori_loop(0, 2, both, 0)
+            lax.fori_loop(0, 2, both, 0, unroll=True)
             part = dot_nt(last[...], back[...])
             parts = [part[:, k * SIDE : (k + 1) * SIDE] for k in range(2)]
         part = jnp.concatenate([part.reshape(n, some * s_lo, SIDE) for part in parts], axis=1)

time: 46.8 us -> 46.8 us (level)
  no operation moved by 1% of the time
where the time goes in v6:
time: 46.8 us; the launch traced here: 46.7 us
  Pallas kernels  45.9 us (98%)
  local copies, waits for them, and re-layouts  0.8 us (2%)
    pallas_call x1, Pallas kernels, shards(): pl.pallas_call(functools.partial(kernel, n, own, s_lo, a_lo, chunks, retu...  45.9 us

profile of v6, /device:TPU:1, one launch (start us, length us, event | category | flops | bytes accessed | tf_op | source)
XLA Modules:
  0.0 46.7 jit_solution(4527573062493658070)
XLA Ops:
  0.0 45.9 %shard_map.82 = bf16[32,32,256]{2,1,0:T(8,128)(2,1)S(1)} custom-call(bf16[2,1024,512]{2,1,0:T(8,128)(2,1)} %filt_hbm.1, bf16[3,1024,256]{2,1,0:T(8,128)(2,1)} %proj_hbm.1, f32[3,3,1024]{2,1,0:T(4,128)} %bitcast.4, f32[8,128]{1,0:T(8,128)} %bitcast.5, bf16[2144,256]{1,0:T(8,128)(2,1)} %constant.8.clone.small_hbm, f32[256,128]{1,0:T(8,128)} %constant.9.clone.twiddle_hbm, ...), custom_call_target="tpu_custom_call" | custom-call | flops 6000000000 | bytes 12000000 | tf_op jit(solution)/shard_map/pallas_call | solution.py:405
  45.9 0.8 %copy.10 = bf16[1024,256]{1,0:T(8,128)(2,1)} copy(bf16[1024,256]{1,0:T(8,128)(2,1)S(1)} %bitcast.3) | data formatting | bytes 1048576
